TPU v7x, 512 devices: a whole 4x4x16 slice. The times are simulated.
512 devices in a mesh: grp: 64 (over z, x_lo, core), freq: 8 (over y, x_hi).
Axes of the slice: x: 4 (x_hi: 2, x_lo: 2; x = x_hi * 2 + x_lo), y: 4, z: 16, core: 2. Of those that a mesh axis runs over, the one named last changes fastest.
Arguments:
- spectra: bfloat16 [8192, 8, 2, 1024], P('grp', None, None, 'freq')
- pairing: int32 [2, 64], replicated, may hold values from 0 to 63, as said below
Outputs:
- correlations: float32 [2, 4096, 128, 256], P(None, ('grp', 'freq'))
Inputs may be any that keep to these rules, and one draw needn't show every extreme that they name: In every round each group's partner is another group, and pairing[r, pairing[r, g]] = g.
All inputs are finite; a program needn't handle non-finite values.
Results may differ from a plain program's by a relative error of at most 0.0055.
Values may be sent and summed in bfloat16 or wider, within the bound.
A program may use at most 64 MiB of HBM per device.

v0:
```python
import math
import jax
import jax.numpy as jnp
from jax import lax
from jax.sharding import PartitionSpec as P

LAGS = 256
VIRTUAL_SOURCES = 64
ROUNDS = 2


def lag_table(bin_count, freq_total):
    bins = jnp.arange(bin_count, dtype=jnp.int32)
    shifts = jnp.arange(LAGS, dtype=jnp.int32) - LAGS // 2
    phase_int = bins[:, None] * shifts[None, :] % (2 * freq_total)
    theta = phase_int.astype(jnp.float32) * (math.pi / freq_total)
    weights = jnp.where(bins == 0, 1.0, 2.0).astype(jnp.float32) / (2.0 * freq_total)
    return jnp.stack(
        [weights[:, None] * jnp.cos(theta), -weights[:, None] * jnp.sin(theta)]
    ).astype(jnp.bfloat16)


def cross_spectra(source_channels, partner):
    src_count, win_count, two_parts, bins = source_channels.shape
    real_left = source_channels.reshape(src_count, win_count * 2, bins)
    imag_left = jnp.stack([source_channels[:, :, 1], -source_channels[:, :, 0]], axis=2).reshape(
        src_count, win_count * 2, bins
    )
    right = partner.reshape(partner.shape[0], win_count * 2, bins)
    real_part = (
        jnp.einsum("skf,ckf->scf", real_left, right, preferred_element_type=jnp.float32) / win_count
    ).astype(jnp.bfloat16)
    imag_part = (
        jnp.einsum("skf,ckf->scf", imag_left, right, preferred_element_type=jnp.float32) / win_count
    ).astype(jnp.bfloat16)
    return jnp.stack([real_part, imag_part], axis=2)


def per_device(spectra, pairing):
    channel_total, win_count, two_parts, freq_local = spectra.shape
    freq_total = freq_local * lax.axis_size("freq")
    group_count = lax.axis_size("grp")
    per_slot = channel_total // group_count
    energy = lax.psum(jnp.sum(jnp.square(spectra.astype(jnp.float32)), axis=(1, 2, 3)), "freq")
    scaling = lax.rsqrt(energy / (win_count * 2 * freq_total) + 1e-06)
    whitened_spectra = (spectra * scaling[:, None, None, None]).astype(jnp.bfloat16)
    spread = lax.all_to_all(
        whitened_spectra.reshape(group_count, per_slot, win_count, two_parts, freq_local),
        "grp",
        split_axis=0,
        concat_axis=0,
        tiled=True,
    )
    source_channels = whitened_spectra[:: channel_total // VIRTUAL_SOURCES]
    shape_back = (channel_total, win_count, two_parts, freq_local)
    partners = []
    for which_round in range(ROUNDS):
        slots = jnp.take(spread, pairing[which_round], axis=0)
        arrived = lax.all_to_all(slots, "grp", split_axis=0, concat_axis=0, tiled=True)
        partners.append(arrived.reshape(shape_back))
    whole_table = lag_table(freq_total, freq_total)
    results = []
    for which_round in range(ROUNDS):
        spectrum = cross_spectra(source_channels, partners[which_round])
        results.append(
            jnp.einsum(
                "scpf,pfl->scl",
                lax.all_to_all(spectrum, "freq", split_axis=0, concat_axis=3, tiled=True),
                whole_table,
                preferred_element_type=jnp.float32,
            )
        )
    return jnp.stack(results)


def solution(mesh):
    placed = (P("grp", None, None, "freq"), P())
    return jax.shard_map(
        per_device,
        mesh=mesh,
        in_specs=placed,
        out_specs=P(None, ("grp", "freq"), None, None),
        check_vma=False,
    )
```

profile of v0, /device:TPU:32, one launch (start us, length us, event | category | flops | bytes accessed | tf_op | source)
XLA Modules:
  0.0 286.4 jit_solution(10637405546343010891)
XLA Ops:
  0.0 2.1 fusion.4
  2.1 24.5 %psum.7 = f32[128]{0:T(128)S(1)} all-reduce(f32[128]{0:T(128)S(1)} %fusion.4), channel_id=1, replica_groups=mesh['grp'=64,'freq'=8] {'freq'}, use_global_device_ids=true, to_apply=%region_1.0 | all-reduce | flops 128 | bytes 1024 | tf_op jit(solution)/shard_map/psum | solution.py:44
  26.6 1.5 fusion.5
  28.1 0.9 copy.18
  29.0 15.8 %all-to-all-start = ((bf16[64,2,8,2,128]{4,2,3,1,0:T(8,128)(2,1)}), bf16[64,2,8,2,128]{4,2,3,1,0:T(8,128)(2,1)S(1)}, u32[]{:S(2)}, u32[]{:S(2)}) async-start(bf16[64,2,8,2,128]{4,2,3,1,0:T(8,128)(2,1)} %bitcast.1), calls=%async_computation | async-start | bytes 1048576 | tf_op jit(solution)/shard_map/all_to_all | solution.py:47
  44.8 0.8 compare_and_fusion.1
  45.6 31.9 %all-to-all-done = bf16[64,2,8,2,128]{4,2,3,1,0:T(8,128)(2,1)S(1)} async-done(((bf16[64,2,8,2,128]{4,2,3,1,0:T(8,128)(2,1)}), bf16[64,2,8,2,128]{4,2,3,1,0:T(8,128)(2,1)S(1)}, u32[]{:S(2)}, u32[]{:S(2)}) %all-to-all-start) | async-done | bytes 524320 | tf_op jit(solution)/shard_map/all_to_all | solution.py:47
  78.1 0.9 broadcast_select_fusion.1
  79.0 5.6 %all-to-all-start.1 = ((bf16[64,2,8,2,128]{4,2,3,1,0:T(8,128)(2,1)}), bf16[64,2,8,2,128]{4,2,3,1,0:T(8,128)(2,1)S(1)}, u32[]{:S(2)}, u32[]{:S(2)}) async-start(bf16[64,2,8,2,128]{4,2,3,1,0:T(8,128)(2,1)} %broadcast_select_fusion.1), calls=%async_computation.1 | async-start | bytes 1048576 | tf_op jit(solution)/shard_map/all_to_all | solution.py:59
  85.3 0.9 broadcast_select_fusion
  86.2 31.1 %all-to-all-done.1 = bf16[64,2,8,2,128]{4,2,3,1,0:T(8,128)(2,1)S(1)} async-done(((bf16[64,2,8,2,128]{4,2,3,1,0:T(8,128)(2,1)}), bf16[64,2,8,2,128]{4,2,3,1,0:T(8,128)(2,1)S(1)}, u32[]{:S(2)}, u32[]{:S(2)}) %all-to-all-start.1) | async-done | bytes 524320 | tf_op jit(solution)/shard_map/all_to_all | solution.py:59
  117.3 5.6 %all-to-all-start.3 = ((bf16[64,2,8,2,128]{4,2,3,1,0:T(8,128)(2,1)}), bf16[64,2,8,2,128]{4,2,3,1,0:T(8,128)(2,1)S(1)}, u32[]{:S(2)}, u32[]{:S(2)}) async-start(bf16[64,2,8,2,128]{4,2,3,1,0:T(8,128)(2,1)} %broadcast_select_fusion), calls=%async_computation.3 | async-start | bytes 1048576 | tf_op jit(solution)/shard_map/all_to_all | solution.py:59
  125.8 0.7 copy.21
  126.5 0.8 fusion.1
  127.3 0.8 fusion
  128.5 4.6 %copy.24 = bf16[64,128,2,128]{1,3,2,0:T(8,128)(2,1)} copy(bf16[64,128,2,128]{1,0,3,2:T(8,128)(2,1)S(1)} %pad_maximum_fusion) | data formatting | bytes 8388608 | tf_op jit(solution)/shard_map/stack | solution.py:36
  133.2 22.5 %all-to-all-done.3 = bf16[64,2,8,2,128]{4,2,3,1,0:T(8,128)(2,1)S(1)} async-done(((bf16[64,2,8,2,128]{4,2,3,1,0:T(8,128)(2,1)}), bf16[64,2,8,2,128]{4,2,3,1,0:T(8,128)(2,1)S(1)}, u32[]{:S(2)}, u32[]{:S(2)}) %all-to-all-start.3) | async-done | bytes 524320 | tf_op jit(solution)/shard_map/all_to_all | solution.py:59
  155.7 4.8 %all-to-all-start.2 = ((bf16[64,128,2,128]{1,3,2,0:T(8,128)(2,1)}), bf16[64,128,2,128]{1,3,2,0:T(8,128)(2,1)}, u32[]{:S(2)}, u32[]{:S(2)}) async-start(bf16[64,128,2,128]{1,3,2,0:T(8,128)(2,1)} %copy.24), calls=%async_computation.2 | async-start | bytes 8388608 | tf_op jit(solution)/shard_map/all_to_all | solution.py:68
  161.7 0.8 fusion.3
  162.4 0.8 fusion.2
  163.6 4.7 %copy.29 = bf16[64,128,2,128]{1,3,2,0:T(8,128)(2,1)} copy(bf16[64,128,2,128]{1,0,3,2:T(8,128)(2,1)S(1)} %pad_maximum_fusion.1) | data formatting | bytes 8388608 | tf_op jit(solution)/shard_map/stack | solution.py:36
  168.3 43.0 %all-to-all-done.2 = bf16[64,128,2,128]{1,3,2,0:T(8,128)(2,1)} async-done(((bf16[64,128,2,128]{1,3,2,0:T(8,128)(2,1)}), bf16[64,128,2,128]{1,3,2,0:T(8,128)(2,1)}, u32[]{:S(2)}, u32[]{:S(2)}) %all-to-all-start.2) | async-done | bytes 4194336 | tf_op jit(solution)/shard_map/all_to_all | solution.py:68
  211.4 4.6 %all-to-all-start.4 = ((bf16[64,128,2,128]{1,3,2,0:T(8,128)(2,1)}), bf16[64,128,2,128]{1,3,2,0:T(8,128)(2,1)}, u32[]{:S(2)}, u32[]{:S(2)}) async-start(bf16[64,128,2,128]{1,3,2,0:T(8,128)(2,1)} %copy.29), calls=%async_computation.4 | async-start | bytes 8388608 | tf_op jit(solution)/shard_map/all_to_all | solution.py:68
  215.9 4.6 %multiply_convert_fusion.5 = (bf16[1,1024,256]{2,1,0:T(8,128)(2,1)S(1)}, bf16[1,1024,256]{2,1,0:T(8,128)(2,1)S(1)}) fusion(s32[256]{0:T(256)S(1)} %iota_add_fusion, f32[1024]{0:T(1024)S(1)} %get-tuple-element.16, f32[1024]{0:T(1024)S(1)} %get-tuple-element.17), kind=kLoop, calls=%fused_computation.27 | loop fusion | flops 4718592 | bytes 1057792 | tf_op jit(solution)/shard_map/convert
  220.5 6.8 %copy.25 = bf16[8,8,128,2,128]{4,0,2,3,1:T(8,128)(2,1)} copy(bf16[8,8,128,2,128]{2,4,3,1,0:T(8,128)(2,1)} %bitcast.9) | data formatting | bytes 8388608 | tf_op jit(solution)/shard_map/all_to_all | solution.py:68
  227.3 7.3 %all_to_all.40 = bf16[8,128,2,1024]{3,1,2,0:T(8,128)(2,1)} reshape(bf16[8,128,2,8,128]{4,3,1,2,0:T(8,128)(2,1)} %bitcast.61) | data formatting | bytes 8388608 | tf_op jit(solution)/shard_map/all_to_all | solution.py:68
  234.6 31.5 %all-to-all-done.4 = bf16[64,128,2,128]{1,3,2,0:T(8,128)(2,1)} async-done(((bf16[64,128,2,128]{1,3,2,0:T(8,128)(2,1)}), bf16[64,128,2,128]{1,3,2,0:T(8,128)(2,1)}, u32[]{:S(2)}, u32[]{:S(2)}) %all-to-all-start.4) | async-done | bytes 4194336 | tf_op jit(solution)/shard_map/all_to_all | solution.py:68
  266.0 6.8 %copy.30 = bf16[8,8,128,2,128]{4,0,2,3,1:T(8,128)(2,1)} copy(bf16[8,8,128,2,128]{2,4,3,1,0:T(8,128)(2,1)} %bitcast.21) | data formatting | bytes 8388608 | tf_op jit(solution)/shard_map/all_to_all | solution.py:68
  272.8 7.3 %all_to_all.45 = bf16[8,128,2,1024]{3,1,2,0:T(8,128)(2,1)} reshape(bf16[8,128,2,8,128]{4,3,1,2,0:T(8,128)(2,1)} %bitcast.62) | data formatting | bytes 8388608 | tf_op jit(solution)/shard_map/all_to_all | solution.py:68
  280.1 3.6 %convolution_bitcast_fusion.1 = f32[1,8,128,256]{3,2,1,0:T(8,128)S(1)} fusion(bf16[8,128,2,1024]{3,1,2,0:T(8,128)(2,1)} %all_to_all.40, bf16[1,1024,256]{2,1,0:T(8,128)(2,1)S(1)} %get-tuple-element.15, bf16[1,1024,256]{2,1,0:T(8,128)(2,1)S(1)} %get-tuple-element.14), kind=kOutput, calls=%fused_computation.17 | convolution fusion | flops 1074266112 | bytes 6291456 | tf_op jit(solution)/shard_map/scpf,pfl->scl/dot_general | solution.py:66
  283.7 1.3 convolution_bitcast_fusion
  285.0 1.5 pad_maximum_fusion.2
  (19 shorter events, 6.1 us)
Async XLA Ops:
  29.0 48.4 %all-to-all-start = ((bf16[64,2,8,2,128]{4,2,3,1,0:T(8,128)(2,1)}), bf16[64,2,8,2,128]{4,2,3,1,0:T(8,128)(2,1)S(1)}, u32[]{:S(2)}, u32[]{:S(2)}) async-start(bf16[64,2,8,2,128]{4,2,3,1,0:T(8,128)(2,1)} %bitcast.1), calls=%async_computation | async-start | bytes 1048576 | tf_op jit(solution)/shard_map/all_to_all | solution.py:47
  79.0 38.3 %all-to-all-start.1 = ((bf16[64,2,8,2,128]{4,2,3,1,0:T(8,128)(2,1)}), bf16[64,2,8,2,128]{4,2,3,1,0:T(8,128)(2,1)S(1)}, u32[]{:S(2)}, u32[]{:S(2)}) async-start(bf16[64,2,8,2,128]{4,2,3,1,0:T(8,128)(2,1)} %broadcast_select_fusion.1), calls=%async_computation.1 | async-start | bytes 1048576 | tf_op jit(solution)/shard_map/all_to_all | solution.py:59
  117.3 38.3 %all-to-all-start.3 = ((bf16[64,2,8,2,128]{4,2,3,1,0:T(8,128)(2,1)}), bf16[64,2,8,2,128]{4,2,3,1,0:T(8,128)(2,1)S(1)}, u32[]{:S(2)}, u32[]{:S(2)}) async-start(bf16[64,2,8,2,128]{4,2,3,1,0:T(8,128)(2,1)} %broadcast_select_fusion), calls=%async_computation.3 | async-start | bytes 1048576 | tf_op jit(solution)/shard_map/all_to_all | solution.py:59
  155.7 55.7 %all-to-all-start.2 = ((bf16[64,128,2,128]{1,3,2,0:T(8,128)(2,1)}), bf16[64,128,2,128]{1,3,2,0:T(8,128)(2,1)}, u32[]{:S(2)}, u32[]{:S(2)}) async-start(bf16[64,128,2,128]{1,3,2,0:T(8,128)(2,1)} %copy.24), calls=%async_computation.2 | async-start | bytes 8388608 | tf_op jit(solution)/shard_map/all_to_all | solution.py:68
  211.4 54.7 %all-to-all-start.4 = ((bf16[64,128,2,128]{1,3,2,0:T(8,128)(2,1)}), bf16[64,128,2,128]{1,3,2,0:T(8,128)(2,1)}, u32[]{:S(2)}, u32[]{:S(2)}) async-start(bf16[64,128,2,128]{1,3,2,0:T(8,128)(2,1)} %copy.29), calls=%async_computation.4 | async-start | bytes 8388608 | tf_op jit(solution)/shard_map/all_to_all | solution.py:68
  280.1 3.6 %copy-start = (bf16[8,128,2,1024]{3,1,2,0:T(8,128)(2,1)S(1)}, bf16[8,128,2,1024]{3,1,2,0:T(8,128)(2,1)}, u32[]{:S(2)}) copy-start(bf16[8,128,2,1024]{3,1,2,0:T(8,128)(2,1)} %all_to_all.45) | copy-start | bytes 12582916
where the time goes:
time: 288 us; the launch traced here: 286 us
  waiting for transfers between devices  160 us (56%)
  local copies, waits for them, and re-layouts  43.2 us (15%)
  starting transfers between devices  36.4 us (13%)
  blocking collectives  24.5 us (9%)
  other arithmetic  14.2 us (5%)
  matrix products  7.98 us (3%)
    all_to_all x2, waiting for transfers between devices, per_device(): lax.all_to_all(spectrum, 'freq', split_axis=0, concat_axis=3, tiled=True)  74.5 us
    all_to_all x2, waiting for transfers between devices, per_device(): lax.all_to_all(slots, 'grp', split_axis=0, concat_axis=0, tiled=True)  53.6 us
    all_to_all x1, waiting for transfers between devices, per_device(): lax.all_to_all(whitened_spectra.reshape(group_count, per_slot, win_count,...  31.9 us
    all_to_all x4, local copies, waits for them, and re-layouts, per_device(): lax.all_to_all(spectrum, 'freq', split_axis=0, concat_axis=3, tiled=True)  28.1 us
    psum x1, blocking collectives, per_device(): lax.psum(jnp.sum(jnp.square(spectra.astype(jnp.float32)), axis=(1, 2, 3))...  24.5 us
    all_to_all x1, starting transfers between devices, per_device(): lax.all_to_all(whitened_spectra.reshape(group_count, per_slot, win_count,...  15.8 us
    all_to_all x2, starting transfers between devices, per_device(): lax.all_to_all(slots, 'grp', split_axis=0, concat_axis=0, tiled=True)  11.2 us
    all_to_all x2, starting transfers between devices, per_device(): lax.all_to_all(spectrum, 'freq', split_axis=0, concat_axis=3, tiled=True)  9.37 us
  transfers between devices with their start and end apart: 5, of which 5 were waited for; matrix products, arithmetic and copies ran while one was open for 11% of the time, Pallas kernels for 0%

commit v1 on v0

--- a/solution.py
+++ b/solution.py
@@ -1,12 +1,29 @@
+import functools
 import math
 import jax
 import jax.numpy as jnp
 from jax import lax
 from jax.sharding import PartitionSpec as P
+from jax.lax import all_to_all, axis_size
 
 LAGS = 256
 VIRTUAL_SOURCES = 64
 ROUNDS = 2
+
+
+def _register_ranges(local, axis_k, which_dim):
+    return jnp.concatenate(
+        all_to_all(
+            jnp.stack(jnp.split(local, axis_size("freq"), axis=axis_k), axis=0),
+            axis_name="freq",
+            split_axis=0,
+            concat_axis=0,
+        ),
+        axis=which_dim,
+    )
+
+
+answer_outputs = functools.partial(_register_ranges, axis_k=0, which_dim=3)
 
 
 def lag_table(bin_count, freq_total):
@@ -65,7 +82,7 @@
         results.append(
             jnp.einsum(
                 "scpf,pfl->scl",
-                lax.all_to_all(spectrum, "freq", split_axis=0, concat_axis=3, tiled=True),
+                answer_outputs(spectrum),
                 whole_table,
                 preferred_element_type=jnp.float32,
             )

time: 288 us -> 274 us (0.951)
  local copies, waits for them, and re-layouts: 43.2 us -> 14.5 us
  other arithmetic: 14.2 us -> 28.5 us
  waiting for transfers between devices: 160 us -> 164 us
    all_to_all x4 -> x0, local copies, waits for them, and re-layouts: 28.1 us -> none  [per_device(): lax.all_to_all(spectrum, 'freq', split_axis=0, concat_axis=3, tiled=True)]
    unnamed x0 -> x14, other arithmetic: none -> 13.1 us
    another operation x2 -> x0, local copies, waits for them, and re-layouts: 9.32 us -> none  [cross_spectra(): return jnp.stack([real_part, imag_part], axis=2)]
    reshape x0 -> x2, local copies, waits for them, and re-layouts: none -> 8.69 us  [_register_ranges(): jnp.concatenate(all_to_all(jnp.stack(jnp.split(local, axis_size('freq'),...]
    all_to_all x2, waiting for transfers between devices: 74.5 us -> 80.8 us  [_register_ranges(): all_to_all(jnp.stack(jnp.split(local, axis_size('freq'), axis=axis_k), ax...]
  transfers between devices with their start and end apart: 5 -> 5, of which waited for: 5 -> 5; matrix products, arithmetic and copies ran while one was open for 11% -> 13% of each run, Pallas kernels for 0% -> 0%
where the time goes in v1:
time: 274 us
  waiting for transfers between devices  164 us (60%)
  starting transfers between devices  36.3 us (13%)
  other arithmetic  28.5 us (10%)
  blocking collectives  24.5 us (9%)
  local copies, waits for them, and re-layouts  14.5 us (5%)
  matrix products  5.71 us (2%)
    all_to_all x2, waiting for transfers between devices, _register_ranges(): all_to_all(jnp.stack(jnp.split(local, axis_size('freq'), axis=axis_k), ax...  80.8 us
    all_to_all x2, waiting for transfers between devices, per_device(): lax.all_to_all(slots, 'grp', split_axis=0, concat_axis=0, tiled=True)  51.1 us
    all_to_all x1, waiting for transfers between devices, per_device(): lax.all_to_all(whitened_spectra.reshape(group_count, per_slot, win_count,...  31.9 us
    psum x1, blocking collectives, per_device(): lax.psum(jnp.sum(jnp.square(spectra.astype(jnp.float32)), axis=(1, 2, 3))...  24.5 us
    all_to_all x1, starting transfers between devices, per_device(): lax.all_to_all(whitened_spectra.reshape(group_count, per_slot, win_count,...  15.8 us
    unnamed x14, other arithmetic  13.1 us
    all_to_all x2, starting transfers between devices, per_device(): lax.all_to_all(slots, 'grp', split_axis=0, concat_axis=0, tiled=True)  11.2 us
    all_to_all x2, starting transfers between devices, _register_ranges(): all_to_all(jnp.stack(jnp.split(local, axis_size('freq'), axis=axis_k), ax...  9.3 us
  transfers between devices with their start and end apart: 5, of which 5 were waited for; matrix products, arithmetic and copies ran while one was open for 13% of the time, Pallas kernels for 0%

profile of v1, /device:TPU:32, one launch (start us, length us, event | category | flops | bytes accessed | tf_op | source)
XLA Modules:
  0.0 273.5 jit_solution(16263813167153066676)
XLA Ops:
  0.0 2.1 fusion.4
  2.1 24.5 %psum.7 = f32[128]{0:T(128)S(1)} all-reduce(f32[128]{0:T(128)S(1)} %fusion.4), channel_id=1, replica_groups=mesh['grp'=64,'freq'=8] {'freq'}, use_global_device_ids=true, to_apply=%region_1.0 | all-reduce | flops 128 | bytes 1024 | tf_op jit(solution)/shard_map/psum | solution.py:61
  26.6 1.5 fusion.5
  29.0 15.8 %all-to-all-start = ((bf16[64,2,8,2,128]{4,2,3,1,0:T(8,128)(2,1)}), bf16[64,2,8,2,128]{4,2,3,1,0:T(8,128)(2,1)S(1)}, u32[]{:S(2)}, u32[]{:S(2)}) async-start(bf16[64,2,8,2,128]{4,2,3,1,0:T(8,128)(2,1)} %bitcast.1), calls=%async_computation | async-start | bytes 1048576 | tf_op jit(solution)/shard_map/all_to_all | solution.py:64
  45.6 31.9 %all-to-all-done = bf16[64,2,8,2,128]{4,2,3,1,0:T(8,128)(2,1)S(1)} async-done(((bf16[64,2,8,2,128]{4,2,3,1,0:T(8,128)(2,1)}), bf16[64,2,8,2,128]{4,2,3,1,0:T(8,128)(2,1)S(1)}, u32[]{:S(2)}, u32[]{:S(2)}) %all-to-all-start) | async-done | bytes 524320 | tf_op jit(solution)/shard_map/all_to_all | solution.py:64
  78.1 0.9 broadcast_select_fusion.1
  79.0 5.6 %all-to-all-start.1 = ((bf16[64,2,8,2,128]{4,2,3,1,0:T(8,128)(2,1)}), bf16[64,2,8,2,128]{4,2,3,1,0:T(8,128)(2,1)S(1)}, u32[]{:S(2)}, u32[]{:S(2)}) async-start(bf16[64,2,8,2,128]{4,2,3,1,0:T(8,128)(2,1)} %broadcast_select_fusion.1), calls=%async_computation.1 | async-start | bytes 1048576 | tf_op jit(solution)/shard_map/all_to_all | solution.py:76
  85.3 0.9 broadcast_select_fusion
  86.2 31.1 %all-to-all-done.1 = bf16[64,2,8,2,128]{4,2,3,1,0:T(8,128)(2,1)S(1)} async-done(((bf16[64,2,8,2,128]{4,2,3,1,0:T(8,128)(2,1)}), bf16[64,2,8,2,128]{4,2,3,1,0:T(8,128)(2,1)S(1)}, u32[]{:S(2)}, u32[]{:S(2)}) %all-to-all-start.1) | async-done | bytes 524320 | tf_op jit(solution)/shard_map/all_to_all | solution.py:76
  117.3 5.6 %all-to-all-start.3 = ((bf16[64,2,8,2,128]{4,2,3,1,0:T(8,128)(2,1)}), bf16[64,2,8,2,128]{4,2,3,1,0:T(8,128)(2,1)S(1)}, u32[]{:S(2)}, u32[]{:S(2)}) async-start(bf16[64,2,8,2,128]{4,2,3,1,0:T(8,128)(2,1)} %broadcast_select_fusion), calls=%async_computation.3 | async-start | bytes 1048576 | tf_op jit(solution)/shard_map/all_to_all | solution.py:76
  128.1 0.9 bitcast_dynamic-update-slice_fusion.13
  130.0 1.0 bitcast_dynamic-update-slice_fusion.11
  131.9 1.0 bitcast_dynamic-update-slice_fusion.9
  132.8 0.9 bitcast_dynamic-update-slice_fusion.8
  134.7 1.0 fusion.29
  135.7 20.0 %all-to-all-done.3 = bf16[64,2,8,2,128]{4,2,3,1,0:T(8,128)(2,1)S(1)} async-done(((bf16[64,2,8,2,128]{4,2,3,1,0:T(8,128)(2,1)}), bf16[64,2,8,2,128]{4,2,3,1,0:T(8,128)(2,1)S(1)}, u32[]{:S(2)}, u32[]{:S(2)}) %all-to-all-start.3) | async-done | bytes 524320 | tf_op jit(solution)/shard_map/all_to_all | solution.py:76
  155.7 4.7 %all-to-all-start.2 = ((bf16[8,8,128,2,128]{2,1,4,3,0:T(8,128)(2,1)}), bf16[8,8,128,2,128]{2,1,4,3,0:T(8,128)(2,1)}, u32[]{:S(2)}, u32[]{:S(2)}) async-start(bf16[8,8,128,2,128]{2,1,4,3,0:T(8,128)(2,1)} %fusion.29), calls=%async_computation.2 | async-start | bytes 8388608 | tf_op jit(solution)/shard_map/all_to_all | solution.py:16
  163.2 1.0 bitcast_dynamic-update-slice_fusion.6
  164.1 1.0 bitcast_dynamic-update-slice_fusion.5
  165.1 0.9 bitcast_dynamic-update-slice_fusion.4
  166.9 0.9 bitcast_dynamic-update-slice_fusion.2
  168.8 0.9 bitcast_dynamic-update-slice_fusion
  169.7 0.9 fusion.27
  170.7 40.6 %all-to-all-done.2 = bf16[8,8,128,2,128]{2,1,4,3,0:T(8,128)(2,1)} async-done(((bf16[8,8,128,2,128]{2,1,4,3,0:T(8,128)(2,1)}), bf16[8,8,128,2,128]{2,1,4,3,0:T(8,128)(2,1)}, u32[]{:S(2)}, u32[]{:S(2)}) %all-to-all-start.2) | async-done | bytes 4194336 | tf_op jit(solution)/shard_map/all_to_all | solution.py:16
  211.3 4.6 %all-to-all-start.4 = ((bf16[8,8,128,2,128]{2,1,4,3,0:T(8,128)(2,1)}), bf16[8,8,128,2,128]{2,1,4,3,0:T(8,128)(2,1)}, u32[]{:S(2)}, u32[]{:S(2)}) async-start(bf16[8,8,128,2,128]{2,1,4,3,0:T(8,128)(2,1)} %fusion.27), calls=%async_computation.4 | async-start | bytes 8388608 | tf_op jit(solution)/shard_map/all_to_all | solution.py:16
  215.9 4.6 %multiply_convert_fusion.5 = (bf16[1,1024,256]{2,1,0:T(8,128)(2,1)S(1)}, bf16[1,1024,256]{2,1,0:T(8,128)(2,1)S(1)}) fusion(s32[256]{0:T(256)S(1)} %iota_add_fusion, f32[1024]{0:T(1024)S(1)} %get-tuple-element.16, f32[1024]{0:T(1024)S(1)} %get-tuple-element.17), kind=kLoop, calls=%fused_computation.53 | loop fusion | flops 4718592 | bytes 1057792 | tf_op jit(solution)/shard_map/convert
  220.5 5.3 %copy.11 = bf16[8,128,2,8,128]{1,4,3,2,0:T(8,128)(2,1)} copy(bf16[8,128,2,8,128]{1,0,4,2,3:T(8,128)(2,1)} %bitcast.17) | data formatting | bytes 8388608 | tf_op jit(solution)/shard_map/reshape | solution.py:15
  225.8 40.2 %all-to-all-done.4 = bf16[8,8,128,2,128]{2,1,4,3,0:T(8,128)(2,1)} async-done(((bf16[8,8,128,2,128]{2,1,4,3,0:T(8,128)(2,1)}), bf16[8,8,128,2,128]{2,1,4,3,0:T(8,128)(2,1)}, u32[]{:S(2)}, u32[]{:S(2)}) %all-to-all-start.4) | async-done | bytes 4194336 | tf_op jit(solution)/shard_map/all_to_all | solution.py:16
  266.0 3.4 %copy.16 = bf16[8,128,2,8,128]{1,4,3,2,0:T(8,128)(2,1)S(1)} copy(bf16[8,128,2,8,128]{1,0,4,2,3:T(8,128)(2,1)} %bitcast.37) | data formatting | bytes 8388608 | tf_op jit(solution)/shard_map/reshape | solution.py:15
  269.4 1.3 convolution_bitcast_fusion.1
  270.7 1.3 convolution_bitcast_fusion
  272.0 1.5 pad_maximum_fusion
  (29 shorter events, 15.4 us)
Async XLA Ops:
  29.0 48.4 %all-to-all-start = ((bf16[64,2,8,2,128]{4,2,3,1,0:T(8,128)(2,1)}), bf16[64,2,8,2,128]{4,2,3,1,0:T(8,128)(2,1)S(1)}, u32[]{:S(2)}, u32[]{:S(2)}) async-start(bf16[64,2,8,2,128]{4,2,3,1,0:T(8,128)(2,1)} %bitcast.1), calls=%async_computation | async-start | bytes 1048576 | tf_op jit(solution)/shard_map/all_to_all | solution.py:64
  79.0 38.3 %all-to-all-start.1 = ((bf16[64,2,8,2,128]{4,2,3,1,0:T(8,128)(2,1)}), bf16[64,2,8,2,128]{4,2,3,1,0:T(8,128)(2,1)S(1)}, u32[]{:S(2)}, u32[]{:S(2)}) async-start(bf16[64,2,8,2,128]{4,2,3,1,0:T(8,128)(2,1)} %broadcast_select_fusion.1), calls=%async_computation.1 | async-start | bytes 1048576 | tf_op jit(solution)/shard_map/all_to_all | solution.py:76
  117.3 38.3 %all-to-all-start.3 = ((bf16[64,2,8,2,128]{4,2,3,1,0:T(8,128)(2,1)}), bf16[64,2,8,2,128]{4,2,3,1,0:T(8,128)(2,1)S(1)}, u32[]{:S(2)}, u32[]{:S(2)}) async-start(bf16[64,2,8,2,128]{4,2,3,1,0:T(8,128)(2,1)} %broadcast_select_fusion), calls=%async_computation.3 | async-start | bytes 1048576 | tf_op jit(solution)/shard_map/all_to_all | solution.py:76
  155.7 55.6 %all-to-all-start.2 = ((bf16[8,8,128,2,128]{2,1,4,3,0:T(8,128)(2,1)}), bf16[8,8,128,2,128]{2,1,4,3,0:T(8,128)(2,1)}, u32[]{:S(2)}, u32[]{:S(2)}) async-start(bf16[8,8,128,2,128]{2,1,4,3,0:T(8,128)(2,1)} %fusion.29), calls=%async_computation.2 | async-start | bytes 8388608 | tf_op jit(solution)/shard_map/all_to_all | solution.py:16
  211.3 54.7 %all-to-all-start.4 = ((bf16[8,8,128,2,128]{2,1,4,3,0:T(8,128)(2,1)}), bf16[8,8,128,2,128]{2,1,4,3,0:T(8,128)(2,1)}, u32[]{:S(2)}, u32[]{:S(2)}) async-start(bf16[8,8,128,2,128]{2,1,4,3,0:T(8,128)(2,1)} %fusion.27), calls=%async_computation.4 | async-start | bytes 8388608 | tf_op jit(solution)/shard_map/all_to_all | solution.py:16
  266.0 3.4 %copy-start = (bf16[8,128,2,8,128]{1,4,3,2,0:T(8,128)(2,1)S(1)}, bf16[8,128,2,8,128]{1,4,3,2,0:T(8,128)(2,1)}, u32[]{:S(2)}) copy-start(bf16[8,128,2,8,128]{1,4,3,2,0:T(8,128)(2,1)} %copy.11) | copy-start | bytes 12582916
